TPU v7x, 32 devices: a whole 2x2x4 slice. The times are simulated.
32 devices in a mesh: seq: 4 (over y, x), dp: 8 (over z, core).
Axes of the slice: x: 2, y: 2, z: 4, core: 2. Of those that a mesh axis runs over, the one named last changes fastest.
Arguments:
- frames: bfloat16 [8, 1024, 1024], P('dp', 'seq'), may hold values from -6 to 6
- segment_ids: int32 [8, 1024], P('dp'), may hold values from 0 to 1, never falling along the last dimension, each value on 1 to 1000 neighbouring positions
- span_starts: int32 [8, 40], P('dp'), may hold values from 0 to 1014
- cotangent: bfloat16 [8, 1024, 1024], P('dp', 'seq'), may hold values from -6 to 6
- attn_master: float32 [1024, 4096], P('seq', 'dp')
- attn_first: float32 [1024, 4096], P('seq', 'dp'), may hold values from -0.00048828125 to 0.00048828125
- attn_second: float32 [1024, 4096], P('seq', 'dp'), may hold values from 3.973643e-11 to 6.3578287e-10
- ffn_master: float32 [4096, 2048], P('seq', 'dp')
- ffn_first: float32 [4096, 2048], P('seq', 'dp'), may hold values from -0.00048828125 to 0.00048828125
- ffn_second: float32 [4096, 2048], P('seq', 'dp'), may hold values from 3.973643e-11 to 6.3578287e-10
- vec_master: float32 [13, 1024], replicated
- vec_first: float32 [13, 1024], replicated, may hold values from -0.00048828125 to 0.00048828125
- vec_second: float32 [13, 1024], replicated, may hold values from 3.973643e-11 to 6.3578287e-10
Outputs:
- output: bfloat16 [8, 1024, 1024], P('dp', 'seq')
- frames_grad: float32 [8, 1024, 1024], P('dp', 'seq')
- grad_norm: float32 [], replicated
- attn_master_new: float32 [1024, 4096], P('seq', 'dp')
- attn_first_new: float32 [1024, 4096], P('seq', 'dp')
- attn_second_new: float32 [1024, 4096], P('seq', 'dp')
- attn_copy: bfloat16 [1024, 4096], P('seq', 'dp')
- ffn_master_new: float32 [4096, 2048], P('seq', 'dp')
- ffn_first_new: float32 [4096, 2048], P('seq', 'dp')
- ffn_second_new: float32 [4096, 2048], P('seq', 'dp')
- ffn_copy: bfloat16 [4096, 2048], P('seq', 'dp')
- vec_master_new: float32 [13, 1024], replicated
- vec_first_new: float32 [13, 1024], replicated
- vec_second_new: float32 [13, 1024], replicated
Inputs may be any that keep to these rules, and one draw needn't show every extreme that they name: `segment_ids`: each group holds 2 utterances one after another, each of 1 to 1000 frames.
All inputs are finite; a program needn't handle non-finite values.
Results may differ from a plain program's by a relative error of at most 0.012.
The roundings to bfloat16 on the way count: a program that leaves them out, or rounds other values in their place, can miss the bound.
Values may be sent and summed in bfloat16 or wider, within the bound.
A program may use at most 128 MiB of HBM per device.

v0:
```python
import functools

import jax
import jax.numpy as jnp
from jax import lax
from jax.experimental import pallas as pl
from jax.experimental.pallas import tpu as pltpu
from jax.sharding import PartitionSpec as P

H = 16
SPAN = 10
STEP = 10

EPS_NORM = 1e-05
BETA_ONE = 0.9
BETA_TWO = 0.999
EPS_ADAM = 1e-08
RATE_ATTN = 0.12
RATE_FFN = 0.03
RATE_VEC = 0.5
DECAY_RATE = 0.01
MAX_NORM = 1.0
NEG_FILL = -1e30

SLABS = 8
LANES = 128
VMEM_LIMIT = 62 * 1024 * 1024
F32 = jnp.float32
BF16 = jnp.bfloat16
MESH = pl.DeviceIdType.MESH


def adam_step(master, first, second, grad, rate, decay):
    first_new = BETA_ONE * first + (1.0 - BETA_ONE) * grad
    second_new = BETA_TWO * second + (1.0 - BETA_TWO) * grad * grad
    first_hat = first_new * (1.0 / (1.0 - BETA_ONE**STEP))
    second_hat = second_new * (1.0 / (1.0 - BETA_TWO**STEP))
    master_new = master - rate * (first_hat / (jnp.sqrt(second_hat) + EPS_ADAM) + decay * master)
    return (master_new, first_new, second_new)


def nn(left, right):
    return lax.dot_general(left, right, (((1,), (0,)), ((), ())), preferred_element_type=F32)


def nt(left, right):
    return lax.dot_general(left, right, (((1,), (1,)), ((), ())), preferred_element_type=F32)


def tn(left, right):
    return lax.dot_general(left, right, (((0,), (0,)), ((), ())), preferred_element_type=F32)


def normalise(source):
    mean_val = jnp.mean(source, axis=-1, keepdims=True)
    centred = source - mean_val
    inv_std = lax.rsqrt(jnp.mean(centred * centred, axis=-1, keepdims=True) + EPS_NORM)
    return centred * inv_std, inv_std


def norm_back(grad_out, normed, inv_std, gain_row):
    scaled = grad_out * gain_row
    inner = (
        scaled
        - jnp.mean(scaled, axis=-1, keepdims=True)
        - normed * jnp.mean(scaled * normed, axis=-1, keepdims=True)
    )
    return inner * inv_std


def col_sum(value):
    return jnp.sum(value, axis=0, keepdims=True)


class Gather:
    def __init__(self, cp, buf, base, place, off, rows):
        self.cp, self.buf, self.b = cp, buf, base
        self.s, self.px, self.py, self.pd = place
        self.off, self.h = off, rows // 2

    def top(self, slot):
        return self.buf.at[slot, pl.ds(self.off, self.h)]

    def bot(self, slot):
        return self.buf.at[slot, pl.ds(self.off + self.h, self.h)]

    def c(self, part, slot, i, to):
        ref = part(slot)
        return self.cp(ref, ref, self.b + i, to)

    def start(self):
        self.c(self.top, self.s, 0, self.px).start()
        self.c(self.bot, self.s, 2, self.py).start()
        self.c(self.bot, self.s, 1, self.px).start()
        self.c(self.top, self.s, 3, self.py).start()

    def relay(self):
        self.c(self.top, self.px, 0, self.px).wait_recv()
        self.c(self.top, self.px, 4, self.py).start()
        self.c(self.bot, self.py, 2, self.py).wait_recv()
        self.c(self.bot, self.py, 5, self.px).start()

    def wait_x(self):
        self.c(self.bot, self.px, 1, self.px).wait_recv()

    def wait_y(self):
        self.c(self.top, self.py, 3, self.py).wait_recv()

    def wait_d(self):
        self.c(self.top, self.pd, 4, self.py).wait_recv()
        self.c(self.bot, self.pd, 5, self.px).wait_recv()

    def sent(self):
        for part, slot, i, to in (
            (self.top, self.s, 0, self.px),
            (self.bot, self.s, 2, self.py),
            (self.bot, self.s, 1, self.px),
            (self.top, self.s, 3, self.py),
            (self.top, self.px, 4, self.py),
            (self.bot, self.py, 5, self.px),
        ):
            self.c(part, slot, i, to).wait_send()


class Scatter:
    def __init__(self, cp, part, in_x, in_y, via_x, via_y, base, place):
        _, px, py, _ = place
        h = in_x.shape[1] // 2
        top, bot = pl.ds(0, h), pl.ds(h, h)
        self.to_x, self.to_y, self.via_x, self.via_y = part(1), part(2), via_x, via_y
        self.top, self.bot = top, bot
        far = part(3)
        self.copies = [
            cp(far.at[:, top], via_x, base, px),
            cp(far.at[:, bot], via_y, base + 1, py),
            cp(self.to_x.at[:, top], in_x.at[:, top], base + 2, px),
            cp(self.to_y.at[:, bot], in_y.at[:, bot], base + 3, py),
            cp(self.to_y.at[:, top], in_y.at[:, top], base + 4, py),
            cp(self.to_x.at[:, bot], in_x.at[:, bot], base + 5, px),
        ]

    def start(self, relation):
        for i in {3: (0, 1), 1: (2,), 2: (3,)}[relation]:
            self.copies[i].start()

    def relay(self):
        for i, ref, via, at in ((0, self.to_y, self.via_x, self.top), (1, self.to_x, self.via_y, self.bot)):
            self.copies[i].wait_recv()
            ref[:, at, :] = (ref[:, at, :].astype(F32) + via[...].astype(F32)).astype(BF16)
            self.copies[4 + i].start()

    def wait(self):
        for i in (2, 3, 4, 5):
            self.copies[i].wait_recv()

    def sent(self):
        for copy in self.copies:
            copy.wait_send()


class Line:
    def __init__(self, cp_dp, buf, base, chip, core, chips):
        self.cp, self.buf, self.b = cp_dp, buf, base
        self.z, self.core, self.n = chip, core, chips

    def c(self, shard, kind, hop):
        ref = self.buf.at[2 * shard + self.core]
        return self.cp(ref, ref, self.b + kind, 2 * (self.z + hop) + self.core)

    def has(self, hop):
        return jnp.logical_and(self.z + hop >= 0, self.z + hop < self.n)

    def across(self, shard):
        ref = self.buf.at[2 * shard + self.core]
        return self.cp(ref, ref, self.b + 6 + shard, 2 * self.z + 1 - self.core)

    def start_first(self):
        for step in (1, -1):
            kind = (1 - step) // 2
            far = self.has(3 * step)

            @pl.when(far)
            def _(kind=kind, step=step):
                self.c(self.z, 2 + kind, 2 * step).start()

            @pl.when(jnp.logical_and(jnp.logical_not(self.has(2 * step)), self.has(step)))
            def _(kind=kind, step=step):
                self.c(self.z, kind, step).start()

        self.across(self.z).start()

    def start_rest(self):
        for step in (1, -1):
            kind = (1 - step) // 2
            far = self.has(3 * step)

            @pl.when(far)
            def _(kind=kind, step=step):
                self.c(self.z, kind, step).start()

            @pl.when(jnp.logical_and(jnp.logical_not(far), self.has(2 * step)))
            def _(kind=kind, step=step):
                self.c(self.z, 2 + kind, 2 * step).start()
                self.c(self.z, kind, step).start()

    def relay(self):
        for kind, hop, on in ((2, -2, 1), (3, 2, -1)):

            @pl.when(jnp.logical_and(self.has(hop), self.has(on)))
            def _(kind=kind, hop=hop, on=on):
                self.c(self.z + hop, kind, hop).wait_recv()
                self.c(self.z + hop, kind + 2, on).start()
                self.across(self.z + hop).start()

    def settle(self):
        for kind, hop, on in ((0, -1, 0), (1, 1, 0), (2, -2, 1), (3, 2, -1), (4, -3, 0), (5, 3, 0)):
            due = self.has(hop)
            if on:
                due = jnp.logical_and(due, jnp.logical_not(self.has(on)))

            @pl.when(due)
            def _(kind=kind, hop=hop):
                self.c(self.z + hop, kind, hop).wait_recv()
                self.across(self.z + hop).start()

        other = 1 - self.core
        for shard in range(self.n):
            ref = self.buf.at[2 * shard + other]
            self.cp(ref, ref, self.b + 6 + shard, 2 * self.z + other).wait_recv()

    def sent(self):
        for shard in range(self.n):
            self.across(shard).wait_send()
        for kind, hop in ((0, 1), (1, -1), (2, 2), (3, -2)):

            @pl.when(self.has(hop))
            def _(kind=kind, hop=hop):
                self.c(self.z, kind, hop).wait_send()

        for kind, hop, on in ((4, -2, 1), (5, 2, -1)):

            @pl.when(jnp.logical_and(self.has(hop), self.has(on)))
            def _(kind=kind, hop=hop, on=on):
                self.c(self.z + hop, kind, on).wait_send()


class LineSum:
    def __init__(self, cp_dp, part, cross, landed, base, chip, core, chips):
        self.cp, self.part, self.cross, self.landed, self.b = cp_dp, part, cross, landed, base
        self.z, self.core, self.n = chip, core, chips

    def mine(self, shard):
        return 2 * shard + self.core

    def has(self, hop):
        return jnp.logical_and(self.z + hop >= 0, self.z + hop < self.n)

    def across(self, shard, half):
        rows = self.part.shape[1] // 2
        at = pl.ds(half * rows, rows)
        src = self.part.at[2 * shard + 1 - self.core, at]
        return self.cp(src, self.cross.at[shard, at], self.b + 6 + 2 * shard + half, 2 * self.z + 1 - self.core)

    def direct(self, kind, hop):
        src = self.part.at[self.mine(self.z + hop)]
        return self.cp(src, self.landed.at[self.z], self.b + kind, 2 * (self.z + hop) + self.core)

    def via(self, kind, hop, step):
        src = self.part.at[self.mine(self.z + hop)]
        return self.cp(src, self.landed.at[self.z + step], self.b + kind, 2 * (self.z + step) + self.core)

    def start(self, half):
        for shard in range(self.n):
            self.across(shard, half).start()

    def add(self, shard, ref, first, rows):
        size = min(256, rows)

        def one(i, carry):
            at = pl.ds(pl.multiple_of(first + i * size, size), size)
            total = self.part[self.mine(shard), at, :].astype(F32) + ref[at, :].astype(F32)
            self.part[self.mine(shard), at, :] = total.astype(BF16)
            return carry

        lax.fori_loop(0, rows // size, one, 0)

    def fold(self, half):
        rows = self.part.shape[1] // 2
        for shard in range(self.n):
            self.across(shard, half).wait_recv()
            self.add(shard, self.cross.at[shard], half * rows, rows)

    def launch(self):
        for step in (1, -1):
            kind = (1 - step) // 2
            far = self.has(3 * step)

            @pl.when(far)
            def _(kind=kind, step=step):
                self.via(4 + kind, 3 * step, step).start()

            @pl.when(jnp.logical_and(jnp.logical_not(far), self.has(step)))
            def _(kind=kind, step=step):
                self.direct(kind, step).start()

    def follow(self):
        for step in (1, -1):
            kind = (1 - step) // 2

            @pl.when(self.has(3 * step))
            def _(kind=kind, step=step):
                self.direct(2 + kind, 2 * step).start()
                self.direct(kind, step).start()

            @pl.when(jnp.logical_and(jnp.logical_not(self.has(3 * step)), self.has(2 * step)))
            def _(kind=kind, step=step):
                @pl.when(self.has(-step))
                def _():
                    here = self.landed.at[self.z]
                    self.cp(here, here, self.b + 4 + kind, 2 * (self.z + step) + self.core).wait_recv()
                    self.add(self.z + 2 * step, here, 0, self.part.shape[1])

                self.direct(2 + kind, 2 * step).start()

    def finish(self, owned):
        owned[...] = self.part[self.mine(self.z)].astype(F32)
        for kind, hop in ((0, -1), (1, 1), (2, -2), (3, 2)):

            @pl.when(self.has(hop))
            def _(kind=kind, hop=hop):
                there = self.landed.at[self.z + hop]
                self.cp(there, there, self.b + kind, 2 * (self.z + hop) + self.core).wait_recv()
                owned[...] += there[...].astype(F32)

    def sent(self):
        for shard in range(self.n):
            for half in range(2):
                self.across(shard, half).wait_send()
        for step in (1, -1):
            kind = (1 - step) // 2
            for hops in (1, 2):

                @pl.when(self.has(hops * step))
                def _(kind=kind, step=step, hops=hops):
                    self.direct(kind + 2 * (hops - 1), hops * step).wait_send()

            @pl.when(self.has(3 * step))
            def _(kind=kind, step=step):
                self.via(4 + kind, 3 * step, step).wait_send()


class Everyone:
    def __init__(self, cp_any, plane, line, base, s, chip, core, chips):
        self.cp, self.plane, self.line, self.b = cp_any, plane, line, base
        self.s, self.z, self.core, self.n = s, chip, core, chips
        self.me = 2 * s + core

    def to_plane(self, o):
        p = lax.rem(self.me + o, 8)
        return self.cp(self.plane.at[self.me], self.plane.at[self.me], self.b + o, p // 2, 2 * self.z + lax.rem(p, 2))

    def from_plane(self, o):
        p = lax.rem(self.me - o + 8, 8)
        return self.cp(self.plane.at[p], self.plane.at[p], self.b + o, p // 2, 2 * self.z + lax.rem(p, 2))

    def to_line(self, o):
        p = lax.rem(self.z + o, self.n)
        return self.cp(self.line.at[self.z], self.line.at[self.z], self.b + 7 + o, self.s, 2 * p + self.core)

    def from_line(self, o):
        p = lax.rem(self.z - o + self.n, self.n)
        return self.cp(self.line.at[p], self.line.at[p], self.b + 7 + o, self.s, 2 * p + self.core)

    def start(self, value):
        self.plane[self.me] = value
        for o in range(1, 8):
            self.to_plane(o).start()

    def middle(self):
        for o in range(1, 8):
            self.from_plane(o).wait_recv()
        total = self.plane[0]
        for p in range(1, 8):
            total = total + self.plane[p]
        self.line[self.z] = total
        for o in range(1, self.n):
            self.to_line(o).start()

    def end(self):
        for o in range(1, self.n):
            self.from_line(o).wait_recv()
        total = self.line[0]
        for p in range(1, self.n):
            total = total + self.line[p]
        return total

    def sent(self):
        for o in range(1, 8):
            self.to_plane(o).wait_send()
        for o in range(1, self.n):
            self.to_line(o).wait_send()


def layer_kernel(inside, chips, *refs):
    refs = list(refs)

    def take(count):
        head = refs[:count]
        del refs[:count]
        return head

    frames, segments, spans, cot, vec, attn_src, ffn_src = take(7)
    if inside:
        out, frames_grad, vec_out, norm_out, attn_owned, ffn_owned = take(6)
    else:
        out, frames_grad, early, late, g_attn, g_ffn = take(6)
        w_attn, w_ffn = attn_src, ffn_src
    fr_g, cot_g, a_g, wp, qa, ka, va, kt, att, b_g, gp_g = take(11)
    act_g = fr_g
    resid, own, part, in_x, in_y, via_x, via_y, in_x2, in_y2, via_x2, via_y2 = take(11)
    gsend, gm, dom, ga_g, gres, dqkv, dk_acc, dv_acc, mask_col, seg_q, seg_k = take(11)
    send_sem, recv_sem, local_sem = take(3)
    if inside:
        w_attn, w_ffn, g_attn, g_ffn, cross_a, cross_f, landed_a, landed_f = take(8)
        early, late, squares, planes, lines, planes_s, lines_s = take(7)
    s = lax.axis_index("seq")
    d = lax.axis_index("dp")
    core = lax.rem(d, 2)
    sib = d + 1 - 2 * core

    def peer(r):
        half = r // 2
        high = lax.rem(s // 2 + half, 2)
        low = lax.rem(lax.rem(s, 2) + (r - 2 * half), 2)
        return 2 * high + low

    px, py, pd = peer(1), peer(2), peer(3)
    place = (s, px, py, pd)

    def cp(src, dst, i, to):
        return pltpu.make_async_remote_copy(
            src_ref=src,
            dst_ref=dst,
            send_sem=send_sem.at[i],
            recv_sem=recv_sem.at[i],
            device_id=(to, d),
            device_id_type=MESH,
        )

    def cp_any(src, dst, i, to_seq, to_dp):
        return pltpu.make_async_remote_copy(
            src_ref=src,
            dst_ref=dst,
            send_sem=send_sem.at[i],
            recv_sem=recv_sem.at[i],
            device_id=(to_seq, to_dp),
            device_id_type=MESH,
        )

    def cp_dp(src, dst, i, to):
        return cp_any(src, dst, i, s, to)

    def cp_sib(src, dst, i):
        return cp_any(src, dst, i, s, sib)


    rows = frames.shape[0]
    width = frames.shape[1]
    local = width // 4
    slab_a = w_attn.shape[2]
    slab_f = w_ffn.shape[2]
    per_a = width // slab_a
    per_f = width // slab_f
    tile = 256
    chunk = 128
    small = 64

    cot_load = pltpu.make_async_copy(cot, cot_g.at[s], local_sem.at[0])
    cot_load.start()
    chip = d // 2
    loads = []
    if inside:
        loads = [pltpu.make_async_copy(attn_src, own.at[:, :slab_a], local_sem.at[1])]
        for i, spot in enumerate((dk_acc, dv_acc)):
            at = slice(i * LANES, (i + 1) * LANES)
            loads.append(pltpu.make_async_copy(ffn_src.at[:, at], spot, local_sem.at[2 + i]))
        for load in loads:
            load.start()

    barrier = pltpu.get_barrier_semaphore()
    if inside:
        for o in range(1, 8):
            p = lax.rem(2 * s + core + o, 8)
            to = (p // 2, 2 * chip + lax.rem(p, 2))
            pl.semaphore_signal(barrier, inc=1, device_id=to, device_id_type=MESH)
        for o in range(1, chips):
            to = (s, 2 * lax.rem(chip + o, chips) + core)
            pl.semaphore_signal(barrier, inc=1, device_id=to, device_id_type=MESH)
        pl.semaphore_wait(barrier, 6 + chips)
    else:
        for to in (px, py, pd):
            pl.semaphore_signal(barrier, inc=1, device_id=(to, d), device_id_type=MESH)
        pl.semaphore_signal(barrier, inc=1, device_id=(s, sib), device_id_type=MESH)
        pl.semaphore_wait(barrier, 4)

    fr_g[s] = frames[...]
    frames_in = Gather(cp, fr_g, 0, place, 0, rows)
    frames_in.start()
    cot_in = Gather(cp, cot_g, 15, place, 0, rows)
    if inside:
        line_a = Line(cp_dp, w_attn, 60, chip, core, chips)
        line_f = Line(cp_dp, w_ffn, 66 + chips, chip, core, chips)
        loads[0].wait()
        w_attn[d] = own[:, :slab_a].astype(BF16)
        line_a.start_first()
    half = rows // 2
    wp_off = pl.multiple_of(core * half, half)
    wp_in = Gather(cp, wp, 6, place, wp_off, half)
    wp_cross = [
        cp_sib(wp.at[p, pl.ds(wp_off, half)], wp.at[p, pl.ds(wp_off, half)], 12 + i) for i, p in enumerate((px, py, pd))
    ]
    early[...] = jnp.zeros_like(early)
    late[...] = jnp.zeros_like(late)

    group = 4 * rows
    position = lax.broadcasted_iota(jnp.int32, (group, spans.shape[1]), 0)
    starts = spans[...]
    covered = jnp.logical_and(position >= starts, position < starts + SPAN)
    mask_col[...] = jnp.max(jnp.where(covered, 1.0, 0.0), axis=1, keepdims=True)
    second = jnp.transpose(jnp.broadcast_to(segments[...].astype(F32), (LANES, group)))
    seg_lane = lax.broadcasted_iota(jnp.int32, (group, LANES), 1)
    fill = jnp.where(seg_lane == 0, second, jnp.where(seg_lane == 1, 1.0 - second, 0.0)) * NEG_FILL
    seg_q[...] = fill.astype(BF16)
    ones = jnp.where(seg_lane < 5, 1.0, 0.0)
    seg_k[...] = jnp.where(seg_lane == 0, 1.0 - second, jnp.where(seg_lane == 1, second, ones)).astype(BF16)
    half = rows // 2

    lane = lax.broadcasted_iota(jnp.int32, (rows, LANES), 1)
    low_head = lane < LANES // 2
    q_bias = vec[2:3, pl.ds(pl.multiple_of(s * local, local), local)]
    v_bias = vec[3:4, pl.ds(pl.multiple_of(s * local, local), local)]

    def weight_rows(first, count, start, size):
        return jnp.concatenate([w_attn[first + i, start : start + size, :] for i in range(count)], axis=1)

    def enter(blk):
        def norm_rows(i, carry):
            at = pl.ds(pl.multiple_of(i * chunk, chunk), chunk)
            at_all = pl.ds(pl.multiple_of(blk * rows + i * chunk, chunk), chunk)
            x = jnp.where(mask_col[at_all, :] > 0.0, vec[8:9, :], fr_g[blk, at, :].astype(F32))
            normed, _ = normalise(x)
            a_g[blk, at, :] = (normed * vec[0:1, :] + vec[1:2, :]).astype(BF16)
            return carry

        lax.fori_loop(0, rows // chunk, norm_rows, 0)

    def project_in(blk):
        a = a_g[blk]
        at_all = pl.ds(pl.multiple_of(blk * rows, rows), rows)
        q = (nt(a, weight_rows(0, per_a, 0, local)) + q_bias).astype(BF16).astype(F32) * 0.125
        for pair in range(2):
            both = q[:, pair * LANES : (pair + 1) * LANES]
            for h in range(2):
                keep = low_head if h == 0 else jnp.logical_not(low_head)
                qa[2 * pair + h, blk, :, :LANES] = jnp.where(keep, both, 0.0).astype(BF16)
                qa[2 * pair + h, blk, :, LANES:] = seg_q[at_all, :]
        k = nt(a, weight_rows(per_a, per_a, 0, local)).astype(BF16)
        for pair in range(2):
            both = k[:, pair * LANES : (pair + 1) * LANES]
            ka[pair, at_all, :LANES] = both
            ka[pair, at_all, LANES:] = seg_k[at_all, :]
            kt[pair, :, at_all] = jnp.transpose(both)
        v = (nt(a, weight_rows(2 * per_a, per_a, 0, local)) + v_bias).astype(BF16)
        for pair in range(2):
            va[pair, at_all, :] = v[:, pair * LANES : (pair + 1) * LANES]

    enter(s)
    if inside:
        for i, spot in enumerate((dk_acc, dv_acc)):
            loads[1 + i].wait()
            w_ffn[d, :, i * LANES : (i + 1) * LANES] = spot[...].astype(BF16)
    if inside:
        line_a.start_rest()
        line_a.relay()
    frames_in.relay()
    frames_in.wait_x()
    enter(px)
    frames_in.wait_y()
    enter(py)
    frames_in.wait_d()
    enter(pd)
    if inside:
        line_a.settle()
        line_f.start_first()
    for i in range(per_a):
        wp[s, :, i * slab_a : (i + 1) * slab_a] = w_attn[3 * per_a + i]
    wp_in.start()
    lax.fori_loop(0, 4, lambda j, carry: (project_in(j), carry)[1], 0)
    cot_load.wait()

    def att_x(j, slot):
        return cp(att.at[slot, j], att.at[slot, j], 21 + j, px)

    def att_y(j, slot):
        return cp(att.at[slot, j], att.at[slot, j], 25 + j, py)

    def att_relay(j, start):
        even = lax.rem(j, 2) == 0

        @pl.when(even)
        def _():
            if start:
                att_x(j, px).wait_recv()
                cp(att.at[px, j], att.at[px, j], 29 + j, py).start()
            else:
                cp(att.at[px, j], att.at[px, j], 29 + j, py).wait_send()

        @pl.when(jnp.logical_not(even))
        def _():
            if start:
                att_y(j, py).wait_recv()
                cp(att.at[py, j], att.at[py, j], 29 + j, px).start()
            else:
                cp(att.at[py, j], att.at[py, j], 29 + j, px).wait_send()

    def attend(j, carry):
        @pl.when(j == 2)
        def _():
            wp_in.relay()
            if inside:
                line_f.start_rest()
                line_f.relay()

        for pair in range(2):
            outs = []
            for h in range(2):
                head = 2 * pair + h
                scores = nt(qa[head, j], ka[pair])
                peak = jnp.max(scores, axis=-1, keepdims=True)
                terms = jnp.exp(scores - peak)
                total = jnp.sum(terms, axis=-1, keepdims=True)
                probs = (terms * (1.0 / total)).astype(BF16)
                outs.append(nn(probs, va[pair]))
                log_total = -(peak + jnp.log(total))
                part_one = log_total.astype(BF16).astype(F32)
                rest = log_total - part_one
                part_two = rest.astype(BF16).astype(F32)
                part_three = rest - part_two
                aug = qa[head, j, :, LANES:].astype(F32)
                aug = jnp.where(lane == 2, part_one, aug)
                aug = jnp.where(lane == 3, part_two, aug)
                aug = jnp.where(lane == 4, part_three, aug)
                qa[head, j, :, LANES:] = aug.astype(BF16)
            att[s, j, :, pair * LANES : (pair + 1) * LANES] = jnp.where(low_head, outs[0], outs[1]).astype(BF16)
        att_x(j, s).start()
        att_y(j, s).start()

        @pl.when(j > 0)
        def _():
            att_relay(j - 1, True)

        return carry

    lax.fori_loop(0, 4, attend, 0)
    wp_in.wait_x()
    wp_cross[0].start()
    wp_in.wait_y()
    wp_cross[1].start()
    wp_in.wait_d()
    wp_cross[2].start()
    att_relay(3, True)
    other_off = pl.multiple_of((1 - core) * half, half)
    for i, p in enumerate((px, py, pd)):
        cp_sib(wp.at[p, pl.ds(other_off, half)], wp.at[p, pl.ds(other_off, half)], 12 + i).wait_recv()

    def project(j, carry):
        @pl.when(j == 1)
        def _():
            cot_in.start()

        even = lax.rem(j, 2) == 0

        @pl.when(even)
        def _():
            att_y(j, py).wait_recv()
            cp(att.at[pd, j], att.at[pd, j], 29 + j, py).wait_recv()

        @pl.when(jnp.logical_not(even))
        def _():
            att_x(j, px).wait_recv()
            cp(att.at[pd, j], att.at[pd, j], 29 + j, px).wait_recv()

        left = jnp.concatenate([att[p, j] for p in range(4)], axis=1)
        for i in range(width // tile):
            right = jnp.concatenate([wp[p, :, i * tile : (i + 1) * tile] for p in range(4)], axis=0)
            own[:, i * tile : (i + 1) * tile] = nn(left, right)

        def norm_rows(i, inner):
            at = pl.ds(pl.multiple_of(i * chunk, chunk), chunk)
            at_all = pl.ds(pl.multiple_of(j * rows + i * chunk, chunk), chunk)
            x = jnp.where(mask_col[at_all, :] > 0.0, vec[8:9, :], fr_g[j, at, :].astype(F32))
            total = x + own[at, :] + vec[4:5, :]

            @pl.when(j == s)
            def _():
                resid[at, :] = total

            normed, _ = normalise(total)
            b_g[j, at, :] = (normed * vec[5:6, :] + vec[6:7, :]).astype(BF16)
            return inner

        lax.fori_loop(0, rows // chunk, norm_rows, 0)
        return carry

    lax.fori_loop(0, 4, project, 0)
    cot_in.relay()
    if inside:
        line_f.settle()
    frames_in.sent()

    def feed(r):
        blk = peer(r)

        def hidden_tile(i, carry):
            at = pl.ds(pl.multiple_of(i * tile, tile), tile)
            w_in = jnp.concatenate([w_ffn[k, at, :] for k in range(per_f)], axis=1)
            w_out = jnp.concatenate([w_ffn[per_f + k, at, :] for k in range(per_f)], axis=1)
            pre = nt(b_g[blk], w_in) + vec[pl.ds(9 + s, 1), at]
            grad_act = nt(cot_g[blk], w_out)
            cdf = 0.5 * (1.0 + lax.erf(pre * 0.7071067811865476))
            act_g[blk, :, at] = (pre * cdf).astype(BF16)
            density = jnp.exp(-0.5 * pre * pre) * 0.3989422804014327
            grad_pre = ((cdf + pre * density) * grad_act).astype(BF16)
            gp_g[blk, :, at] = grad_pre
            early[pl.ds(4 + s, 1), at] += col_sum(grad_pre.astype(F32))
            return carry

        lax.fori_loop(0, w_ffn.shape[1] // tile, hidden_tile, 0)
        left = gp_g[blk]
        for k in range(per_f):
            at = slice(k * slab_f, (k + 1) * slab_f)
            value = nn(left, w_ffn[k])
            if r == 0:
                own[:, at] = value
            else:
                part[r - 1, k] = value.astype(BF16)

    sum_b = Scatter(cp, lambda r: part.at[r - 1], in_x, in_y, via_x, via_y, 33, place)
    cot_in.wait_d()
    feed(3)
    sum_b.start(3)
    cot_in.wait_x()
    feed(1)
    sum_b.start(1)
    cot_in.wait_y()
    feed(2)
    sum_b.start(2)
    sum_b.relay()
    feed(0)

    def ffn_grads(i, carry):
        at = pl.ds(pl.multiple_of(i * tile, tile), tile)
        for left, right, first in ((gp_g, b_g, 0), (act_g, cot_g, per_f)):
            turned = jnp.transpose(jnp.concatenate([left[p, :, at] for p in range(4)], axis=0))
            for k in range(per_f):
                cols = jnp.concatenate([right[p, :, k * slab_f : (k + 1) * slab_f] for p in range(4)], axis=0)
                g_ffn[first + k, at, :] = nn(turned, cols).astype(BF16)
        return carry

    f_tiles = w_ffn.shape[1] // tile
    if inside:
        sum_f = LineSum(cp_dp, g_ffn, cross_f, landed_f, 72 + 2 * chips, chip, core, chips)
        sum_g = LineSum(cp_dp, g_attn, cross_a, landed_a, 78 + 4 * chips, chip, core, chips)
        all_early = Everyone(cp_any, planes.at[0], lines.at[0], 84 + 6 * chips, s, chip, core, chips)
        all_late = Everyone(cp_any, planes.at[1], lines.at[1], 91 + 7 * chips, s, chip, core, chips)
        all_squares = Everyone(cp_any, planes_s, lines_s, 98 + 8 * chips, s, chip, core, chips)
    def ffn_grads_sent(i, carry):
        if inside:

            @pl.when(i == f_tiles // 2)
            def _():
                sum_f.start(0)

        return ffn_grads(i, carry)

    lax.fori_loop(0, f_tiles, ffn_grads_sent, 0)
    if inside:
        sum_f.start(1)
    if inside:
        sum_f.fold(0)
        sum_f.fold(1)
        sum_f.launch()

    def out_part(blk, k):
        return nn(act_g[blk], w_ffn[per_f + k])

    for j in range(4):
        att_x(j, s).wait_send()
        att_y(j, s).wait_send()
        att_relay(j, False)
    sum_o = Scatter(cp, lambda r: att.at[peer(r)], in_x2, in_y2, via_x2, via_y2, 48, place)
    for r in (3, 1, 2):
        for k in range(per_f):
            att[peer(r), k] = out_part(peer(r), k).astype(BF16)
    sum_b.wait()
    sum_o.start(3)

    def landed(from_x, from_y, at):
        tiles = range(from_x.shape[0])
        return jnp.concatenate([from_x[t, at, :].astype(F32) + from_y[t, at, :].astype(F32) for t in tiles], axis=1)

    def back_two(i, carry):
        at = pl.ds(pl.multiple_of(i * small, small), small)
        grad_b = own[at, :] + landed(in_x, in_y, at)
        normed, inv_std = normalise(resid[at, :])
        grad_y = cot_g[s, at, :].astype(F32)
        grad_resid = grad_y + norm_back(grad_b, normed, inv_std, vec[5:6, :])
        gres[at, :] = grad_resid
        low = grad_resid.astype(BF16)
        ga_g[s, at, :] = low
        early[0:1, :] += col_sum(low.astype(F32))
        early[1:2, :] += col_sum(grad_b * normed)
        early[2:3, :] += col_sum(grad_b)
        early[3:4, :] += col_sum(grad_y)
        return carry

    lax.fori_loop(0, rows // small, back_two, 0)

    for i, r in enumerate((3, 1, 2)):
        gsend[r] = nt(ga_g[s], wp[peer(r)]).astype(BF16)
        cp(gsend.at[r], gm.at[s], 39 + i, peer(r)).start()
    gm[s] = nt(ga_g[s], wp[s]).astype(BF16)
    ga_in = Gather(cp, ga_g, 42, place, 0, rows)
    ga_in.start()
    sum_b.sent()

    def spread(j):
        for pair in range(2):
            both = gm[j, :, pair * LANES : (pair + 1) * LANES].astype(F32)
            dom[2 * pair, j] = jnp.where(low_head, both, 0.0).astype(BF16)
            dom[2 * pair + 1, j] = jnp.where(low_head, 0.0, both).astype(BF16)

    def arrive(i, r):
        cp(gsend.at[r], gm.at[peer(r)], 39 + i, peer(r)).wait_recv()
        spread(peer(r))

    spread(s)

    def back_pair(pair, first, second):
        dk_acc[...] = jnp.zeros_like(dk_acc)
        dv_acc[...] = jnp.zeros_like(dv_acc)

        def back_block(r, carry):
            j = peer(r)
            for at_block, task in ((1, first), (3, second)):
                if task is not None:
                    pl.when(r == at_block)(task)
            sides = []
            for h in range(2):
                head = 2 * pair + h
                probs = jnp.exp(nt(ka[pair], qa[head, j]))
                grad_probs = nt(va[pair], dom[head, j])
                delta = jnp.sum(probs * grad_probs, axis=0, keepdims=True)
                grad_scores = (probs * (grad_probs - delta)).astype(BF16)
                dv_acc[...] += nn(probs.astype(BF16), dom[head, j])
                dk_acc[...] += nn(grad_scores, qa[head, j, :, :LANES])
                sides.append(nn(kt[pair], grad_scores))
            half_lane = LANES // 2
            turned = jnp.concatenate([sides[0][:half_lane], sides[1][half_lane:]], axis=0)
            dqkv[0, j, :, pair * LANES : (pair + 1) * LANES] = (jnp.transpose(turned) * 0.125).astype(BF16)
            return carry

        lax.fori_loop(0, 4, back_block, 0)
        for j in range(4):
            at = slice(j * rows, (j + 1) * rows)
            dqkv[1, j, :, pair * LANES : (pair + 1) * LANES] = dk_acc[at, :].astype(BF16)
            dqkv[2, j, :, pair * LANES : (pair + 1) * LANES] = dv_acc[at, :].astype(BF16)

    def after_own():
        arrive(1, 1)
        arrive(2, 2)

    def after_near():
        arrive(0, 3)
        if inside:
            sum_f.follow()
            all_early.start(early[...])

    back_pair(0, after_own, after_near)
    back_pair(1, None, ga_in.relay)

    sum_a = Scatter(cp, lambda r: part.at[r - 1], in_x, in_y, via_x, via_y, 54, place)

    def grad_in(r):
        blk = peer(r)
        left = jnp.concatenate([dqkv[c, blk] for c in range(3)], axis=1)
        for k in range(per_a):
            at = slice(k * slab_a, (k + 1) * slab_a)
            right = jnp.concatenate([w_attn[c * per_a + k] for c in range(3)], axis=0)
            value = nn(left, right)
            if r == 0:
                own[:, at] = value
            else:
                per_tile = slab_a // tile
                for t in range(per_tile):
                    part[r - 1, k * per_tile + t] = value[:, t * tile : (t + 1) * tile].astype(BF16)

    for r in (3, 1, 2):
        grad_in(r)
        sum_a.start(r)
    grad_in(0)

    my_cols = pl.ds(pl.multiple_of(s * local, local), local)
    for j in range(4):
        late[2:3, my_cols] += col_sum(dqkv[0, j].astype(F32))
        late[3:4, my_cols] += col_sum(dqkv[2, j].astype(F32))

    def attn_grads(c):
        turned = jnp.transpose(jnp.concatenate([dqkv[c, p] for p in range(4)], axis=0))
        for k in range(per_a):
            cols = jnp.concatenate([a_g[p, :, k * slab_a : (k + 1) * slab_a] for p in range(4)], axis=0)
            g_attn[c * per_a + k] = nn(turned, cols).astype(BF16)

    attn_grads(0)
    attn_grads(1)
    attn_grads(2)
    ga_in.wait_x()
    ga_in.wait_y()
    ga_in.wait_d()
    turned = jnp.transpose(jnp.concatenate([att[s, p] for p in range(4)], axis=0))
    for k in range(per_a):
        cols = jnp.concatenate([ga_g[p, :, k * slab_a : (k + 1) * slab_a] for p in range(4)], axis=0)
        g_attn[3 * per_a + k] = nn(turned, cols).astype(BF16)

    if inside:
        sum_g.start(0)
        sum_g.start(1)
    sum_a.relay()
    if inside:
        sum_g.fold(0)
        sum_g.fold(1)
        sum_g.launch()
    if inside:
        sum_f.finish(ffn_owned)
        ffn_squares = col_sum(ffn_owned[...] * ffn_owned[...])
        squares[...] = jnp.zeros_like(squares)
        sum_g.follow()
    sum_a.wait()
    sum_o.start(1)
    sum_o.start(2)
    sum_o.relay()

    def back_one(i, carry):
        at = pl.ds(pl.multiple_of(i * small, small), small)
        at_all = pl.ds(pl.multiple_of(s * rows + i * small, small), small)
        grad_a = own[at, :] + landed(in_x, in_y, at)
        masked = mask_col[at_all, :] > 0.0
        normed, inv_std = normalise(jnp.where(masked, vec[8:9, :], frames[at, :].astype(F32)))
        grad_x = gres[at, :] + norm_back(grad_a, normed, inv_std, vec[0:1, :])
        frames_grad[at, :] = jnp.where(masked, 0.0, grad_x)
        late[0:1, :] += col_sum(grad_a * normed)
        late[1:2, :] += col_sum(grad_a)
        late[4:5, :] += col_sum(jnp.where(masked, grad_x, 0.0))
        return carry

    lax.fori_loop(0, rows // small, back_one, 0)
    if inside:
        all_late.start(late[...])
        all_early.middle()
        sum_g.finish(attn_owned)
        attn_squares = col_sum(attn_owned[...] * attn_owned[...])
        owned_squares = sum(attn_squares[:, i * LANES : (i + 1) * LANES] for i in range(slab_a // LANES))
        owned_squares += sum(ffn_squares[:, i * LANES : (i + 1) * LANES] for i in range(slab_f // LANES))
        squares[0:1, :] = owned_squares
        all_squares.start(squares[...])
        all_late.middle()
        whole_early = all_early.end()
        all_squares.middle()
        whole_late = all_late.end()
        vec_out[0:4, :] = whole_late[0:4]
        vec_out[4:8, :] = whole_early[0:4]
        vec_out[8:9, :] = whole_late[4:5]
        vec_out[9:13, :] = whole_early[4:8]
        vec_square = col_sum(vec_out[...] * vec_out[...])

    sum_o.wait()
    for k in range(per_f):
        at = slice(k * slab_f, (k + 1) * slab_f)
        total = out_part(s, k) + resid[:, at] + in_x2[k].astype(F32) + in_y2[k].astype(F32) + vec[7:8, at]
        out[:, at] = total.astype(BF16)

    if inside:
        whole_squares = all_squares.end()
        total = jnp.sum(whole_squares[0:1], axis=1, keepdims=True) + jnp.sum(vec_square, axis=1, keepdims=True)
        norm_out[...] = jnp.broadcast_to(jnp.sqrt(total), norm_out.shape)
        line_a.sent()
        line_f.sent()
        sum_f.sent()
        sum_g.sent()
        all_early.sent()
        all_late.sent()
        all_squares.sent()

    wp_in.sent()
    for copy in wp_cross:
        copy.wait_send()
    cot_in.sent()

    for i, r in enumerate((3, 1, 2)):
        cp(gsend.at[r], gm.at[s], 39 + i, peer(r)).wait_send()
    ga_in.sent()
    sum_a.sent()
    sum_o.sent()


def run_layer(frames, segments, spans, cot, vec, attn_src, ffn_src, inside, chips):
    rows, width = frames.shape
    group = 4 * rows
    local = width // 4
    slab_count = 2 * chips if inside else SLABS
    hidden = ffn_src.shape[0] if inside else ffn_src.shape[1]
    attn_shape = (slab_count, local, attn_src.shape[-1])
    ffn_shape = (slab_count, hidden, ffn_src.shape[-1])
    vmem = pl.BlockSpec(memory_space=pltpu.VMEM)
    anywhere = pl.BlockSpec(memory_space=pl.ANY)
    source = anywhere if inside else vmem
    block = (4, rows, width)
    sums = (8, width)
    scratch = [
        pltpu.VMEM(block, BF16),
        pltpu.VMEM(block, BF16),
        pltpu.VMEM(block, BF16),
        pltpu.VMEM((4, local, width), BF16),
        pltpu.VMEM((4, 4, rows, 2 * LANES), BF16),
        pltpu.VMEM((2, group, 2 * LANES), BF16),
        pltpu.VMEM((2, group, LANES), BF16),
        pltpu.VMEM((2, LANES, group), BF16),
        pltpu.VMEM((4, 4, rows, local), BF16),
        pltpu.VMEM(block, BF16),
        pltpu.VMEM((4, rows, hidden), BF16),
        pltpu.VMEM((rows, width), F32),
        pltpu.VMEM((rows, width), F32),
        pltpu.VMEM((3, 4, rows, local), BF16),
        pltpu.VMEM((4, rows, local), BF16),
        pltpu.VMEM((4, rows, local), BF16),
        pltpu.VMEM((4, rows // 2, local), BF16),
        pltpu.VMEM((4, rows // 2, local), BF16),
        pltpu.VMEM((4, rows, local), BF16),
        pltpu.VMEM((4, rows, local), BF16),
        pltpu.VMEM((4, rows // 2, local), BF16),
        pltpu.VMEM((4, rows // 2, local), BF16),
        pltpu.VMEM((4, rows, local), BF16),
        pltpu.VMEM((4, rows, local), BF16),
        pltpu.VMEM((4, 4, rows, LANES), BF16),
        pltpu.VMEM(block, BF16),
        pltpu.VMEM((rows, width), F32),
        pltpu.VMEM((3, 4, rows, local), BF16),
        pltpu.VMEM((group, LANES), F32),
        pltpu.VMEM((group, LANES), F32),
        pltpu.VMEM((group, 1), F32),
        pltpu.VMEM((group, LANES), BF16),
        pltpu.VMEM((group, LANES), BF16),
    ]
    sem_count = 106 + 9 * chips if inside else 60
    scratch += [pltpu.SemaphoreType.DMA((sem_count,)), pltpu.SemaphoreType.DMA((sem_count,))]
    scratch.append(pltpu.SemaphoreType.DMA((4,)))
    if inside:
        scratch += [
            pltpu.VMEM(attn_shape, BF16),
            pltpu.VMEM(ffn_shape, BF16),
            pltpu.VMEM(attn_shape, BF16),
            pltpu.VMEM(ffn_shape, BF16),
            pltpu.VMEM((chips, *attn_shape[1:]), BF16),
            pltpu.VMEM((chips, *ffn_shape[1:]), BF16),
            pltpu.VMEM((chips, *attn_shape[1:]), BF16),
            pltpu.VMEM((chips, *ffn_shape[1:]), BF16),
            pltpu.VMEM(sums, F32),
            pltpu.VMEM(sums, F32),
            pltpu.VMEM((8, LANES), F32),
            pltpu.VMEM((2, 8, *sums), F32),
            pltpu.VMEM((2, chips, *sums), F32),
            pltpu.VMEM((8, 8, LANES), F32),
            pltpu.VMEM((chips, 8, LANES), F32),
        ]
        last = (
            jax.ShapeDtypeStruct(vec.shape, F32),
            jax.ShapeDtypeStruct((8, LANES), F32),
            jax.ShapeDtypeStruct(attn_shape[1:], F32),
            jax.ShapeDtypeStruct(ffn_shape[1:], F32),
        )
    else:
        last = (
            jax.ShapeDtypeStruct(sums, F32),
            jax.ShapeDtypeStruct(sums, F32),
            jax.ShapeDtypeStruct(attn_shape, BF16),
            jax.ShapeDtypeStruct(ffn_shape, BF16),
        )
    return pl.pallas_call(
        functools.partial(layer_kernel, inside, chips),
        out_shape=(jax.ShapeDtypeStruct((rows, width), BF16), jax.ShapeDtypeStruct((rows, width), F32), *last),
        in_specs=[vmem, vmem, vmem, anywhere, vmem, source, source],
        out_specs=(vmem,) * 6,
        scratch_shapes=scratch,
        compiler_params=pltpu.CompilerParams(
            collective_id=0, has_side_effects=True, vmem_limit_bytes=VMEM_LIMIT
        ),
    )(frames, segments, spans, cot, vec, attn_src, ffn_src)


def adam_kernel(norm, *refs):
    clip = jnp.minimum(1.0, MAX_NORM / (norm[0, 0] + 1e-06))
    attn, ffn, vec = refs[0:4], refs[4:8], refs[8:12]
    attn_to, ffn_to, vec_to, norm_to = refs[12:16], refs[16:20], refs[20:23], refs[23]

    def update(source, target, rate, decay):
        master, first, second, grad = (ref[...] for ref in source)
        for ref, value in zip(target, adam_step(master, first, second, grad * clip, rate, decay)):
            ref[...] = value
        if len(target) > 3:
            target[3][...] = target[0][...].astype(BF16)

    update(attn, attn_to, RATE_ATTN, DECAY_RATE)
    update(ffn, ffn_to, RATE_FFN, DECAY_RATE)

    @pl.when(pl.program_id(0) == 0)
    def _():
        update(vec, vec_to, RATE_VEC, 0.0)
        norm_to[0, 0] = norm[0, 0]


def run_adam(norm, attn, ffn, vec):
    steps = 2

    def split(array):
        return pl.BlockSpec((array.shape[0] // steps, array.shape[1]), lambda i: (i, 0))

    whole = pl.BlockSpec(vec[0].shape, lambda i: (0, 0))
    scalar = pl.BlockSpec(memory_space=pltpu.SMEM)

    def shapes(array, copy):
        types = (F32, F32, F32, BF16) if copy else (F32, F32, F32)
        return tuple(jax.ShapeDtypeStruct(array.shape, t) for t in types)

    return pl.pallas_call(
        adam_kernel,
        grid=(steps,),
        out_shape=(
            *shapes(attn[0], True),
            *shapes(ffn[0], True),
            *shapes(vec[0], False),
            jax.ShapeDtypeStruct((1, 1), F32),
        ),
        in_specs=[scalar] + [split(attn[0])] * 4 + [split(ffn[0])] * 4 + [whole] * 4,
        out_specs=(*[split(attn[0])] * 4, *[split(ffn[0])] * 4, *[whole] * 3, scalar),
        compiler_params=pltpu.CompilerParams(vmem_limit_bytes=VMEM_LIMIT),
    )(norm, *attn, *ffn, *vec)


def per_device(
    frames,
    segment_ids,
    span_starts,
    cotangent,
    attn_master,
    attn_first,
    attn_second,
    ffn_master,
    ffn_first,
    ffn_second,
    vec_master,
    vec_first,
    vec_second,
):
    dp_count = lax.axis_size("dp")

    def gather_slabs(master):
        shard = master.astype(BF16)
        whole = lax.all_gather(shard, "dp", axis=1, tiled=True)
        return whole.reshape(shard.shape[0], SLABS, -1).transpose(1, 0, 2)

    inside = attn_master.shape[1] % 256 == 0 and ffn_master.shape[1] % 256 == 0 and dp_count in (4, 8)
    head = (frames[0], segment_ids, span_starts, cotangent[0], vec_master)
    if inside:
        output, frames_grad, vec_grad, norm, attn_owned, ffn_owned = run_layer(
            *head, attn_master, ffn_master, True, dp_count // 2
        )
    else:
        output, frames_grad, early, late, g_attn, g_ffn = run_layer(
            *head, gather_slabs(attn_master), gather_slabs(ffn_master), False, dp_count // 2
        )
        vec_local = jnp.concatenate([late[0:4], early[0:4], late[4:5], early[4:8]], axis=0)

        def scatter_slabs(slabs):
            whole = slabs.astype(F32).transpose(1, 0, 2).reshape(slabs.shape[1], -1)
            return lax.psum_scatter(whole, "dp", scatter_dimension=1, tiled=True)

        attn_owned = scatter_slabs(g_attn)
        ffn_owned = scatter_slabs(g_ffn)
        owned_squares = jnp.sum(attn_owned * attn_owned) + jnp.sum(ffn_owned * ffn_owned)
        vec_grad, total_squares = lax.psum((vec_local, owned_squares), ("seq", "dp"))
        norm = jnp.broadcast_to(jnp.sqrt(total_squares + jnp.sum(vec_grad * vec_grad)), (8, LANES))
    updated = run_adam(
        norm,
        (attn_master, attn_first, attn_second, attn_owned),
        (ffn_master, ffn_first, ffn_second, ffn_owned),
        (vec_master, vec_first, vec_second, vec_grad),
    )
    return (output[None], frames_grad[None], updated[-1].reshape(()), *updated[:-1])


def solution(mesh):
    return jax.shard_map(
        per_device,
        mesh=mesh,
        in_specs=(
            P("dp", "seq", None),
            P("dp", None),
            P("dp", None),
            P("dp", "seq", None),
            P("seq", "dp"),
            P("seq", "dp"),
            P("seq", "dp"),
            P("seq", "dp"),
            P("seq", "dp"),
            P("seq", "dp"),
            P(),
            P(),
            P(),
        ),
        out_specs=(
            P("dp", "seq", None),
            P("dp", "seq", None),
            P(),
            P("seq", "dp"),
            P("seq", "dp"),
            P("seq", "dp"),
            P("seq", "dp"),
            P("seq", "dp"),
            P("seq", "dp"),
            P("seq", "dp"),
            P("seq", "dp"),
            P(),
            P(),
            P(),
        ),
        check_vma=False,
    )
```

profile of v0, /device:TPU:0, one launch (start us, length us, event | category | flops | bytes accessed | tf_op | source)
XLA Modules:
  0.0 182.2 jit_solution(17190839177193864208)
XLA Ops:
  0.6 172.5 %shard_map.236 = (bf16[256,1024]{1,0:T(8,128)(2,1)}, f32[256,1024]{1,0:T(8,128)}, f32[13,1024]{1,0:T(8,128)}, f32[8,128]{1,0:T(8,128)}, f32[256,512]{1,0:T(8,128)}, /*index=5*/f32[1024,256]{1,0:T(8,128)}) custom-call(bf16[256,1024]{1,0:T(8,128)(2,1)} %bitcast.7, s32[1,1024]{1,0:T(1,128)} %refs_1_.2, s32[1,40]{1,0:T(1,128)} %refs_2_.2, ...), custom_call_target="tpu_custom_call" | custom-call | tf_op jit(solution)/shard_map/pallas_call | solution.py:1098
  173.1 0.0 copy-start.1
  173.1 6.7 %shard_map.237 = (f32[256,512]{1,0:T(8,128)}, f32[256,512]{1,0:T(8,128)}, f32[256,512]{1,0:T(8,128)}, bf16[256,512]{1,0:T(8,128)(2,1)}, f32[1024,256]{1,0:T(8,12...) custom-call(f32[8,128]{1,0:T(8,128)} %get-tuple-element.34.norm, ...), custom_call_target="tpu_custom_call" | custom-call | tf_op jit(solution)/shard_map/pallas_call | solution.py:1144
  179.8 0.0 copy-start
  179.8 0.0 copy-done.1
  179.8 0.8 copy.29
  180.6 0.6 copy-done
  181.2 1.0 copy.30
Async XLA Ops:
  173.1 6.7 %copy-start.1 = (bf16[256,1024]{1,0:T(8,128)(2,1)S(1)}, bf16[256,1024]{1,0:T(8,128)(2,1)}, u32[]{:S(2)}) copy-start(bf16[256,1024]{1,0:T(8,128)(2,1)} %get-tuple-element.32) | copy-start | bytes 1572868
  179.8 1.4 copy-start
where the time goes:
time: 182 us
  Pallas kernels  179 us (98%)
  local copies, waits for them, and re-layouts  2.37 us (1%)
    pallas_call x1, Pallas kernels, run_layer(): pl.pallas_call(functools.partial(layer_kernel, inside, chips), out_shape=...  172 us
    pallas_call x1, Pallas kernels, run_adam(): pl.pallas_call(adam_kernel, grid=(steps,), out_shape=(*shapes(attn[0], Tr...  6.69 us

commit v1 on v0

--- a/solution.py
+++ b/solution.py
@@ -1110,7 +1110,10 @@
 def adam_kernel(norm, *refs):
     clip = jnp.minimum(1.0, MAX_NORM / (norm[0, 0] + 1e-06))
     attn, ffn, vec = refs[0:4], refs[4:8], refs[8:12]
-    attn_to, ffn_to, vec_to, norm_to = refs[12:16], refs[16:20], refs[20:23], refs[23]
+    passed, refs = refs[12:14], refs[14:]
+    attn_to, ffn_to, vec_to, norm_to, passed_to = refs[0:4], refs[4:8], refs[8:11], refs[11], refs[12:14]
+    for source, target in zip(passed, passed_to):
+        target[...] = source[...]
 
     def update(source, target, rate, decay):
         master, first, second, grad = (ref[...] for ref in source)
@@ -1128,7 +1131,7 @@
         norm_to[0, 0] = norm[0, 0]
 
 
-def run_adam(norm, attn, ffn, vec):
+def run_adam(norm, attn, ffn, vec, passed):
     steps = 2
 
     def split(array):
@@ -1149,11 +1152,12 @@
             *shapes(ffn[0], True),
             *shapes(vec[0], False),
             jax.ShapeDtypeStruct((1, 1), F32),
+            *[jax.ShapeDtypeStruct(array.shape, array.dtype) for array in passed],
         ),
-        in_specs=[scalar] + [split(attn[0])] * 4 + [split(ffn[0])] * 4 + [whole] * 4,
-        out_specs=(*[split(attn[0])] * 4, *[split(ffn[0])] * 4, *[whole] * 3, scalar),
+        in_specs=[scalar] + [split(attn[0])] * 4 + [split(ffn[0])] * 4 + [whole] * 4 + [split(array) for array in passed],
+        out_specs=(*[split(attn[0])] * 4, *[split(ffn[0])] * 4, *[whole] * 3, scalar, *[split(array) for array in passed]),
         compiler_params=pltpu.CompilerParams(vmem_limit_bytes=VMEM_LIMIT),
-    )(norm, *attn, *ffn, *vec)
+    )(norm, *attn, *ffn, *vec, *passed)
 
 
 def per_device(
@@ -1204,8 +1208,9 @@
         (attn_master, attn_first, attn_second, attn_owned),
         (ffn_master, ffn_first, ffn_second, ffn_owned),
         (vec_master, vec_first, vec_second, vec_grad),
+        (output, frames_grad),
     )
-    return (output[None], frames_grad[None], updated[-1].reshape(()), *updated[:-1])
+    return (updated[-2][None], updated[-1][None], updated[-3].reshape(()), *updated[:-3])
 
 
 def solution(mesh):

time: 182 us -> 181 us (level)
  local copies, waits for them, and re-layouts: 2.37 us -> 0 us
    unnamed x6 -> x0, local copies, waits for them, and re-layouts: 2.37 us -> none
where the time goes in v1:
time: 181 us
  Pallas kernels  180 us (99%)
    pallas_call x1, Pallas kernels, run_layer(): pl.pallas_call(functools.partial(layer_kernel, inside, chips), out_shape=...  172 us
    pallas_call x1, Pallas kernels, run_adam(): pl.pallas_call(adam_kernel, grid=(steps,), out_shape=(*shapes(attn[0], Tr...  7.24 us

profile of v1, /device:TPU:0, one launch (start us, length us, event | category | flops | bytes accessed | tf_op | source)
XLA Modules:
  0.0 180.5 jit_solution(6607107326757783853)
XLA Ops:
  0.6 172.5 %shard_map.236 = (bf16[256,1024]{1,0:T(8,128)(2,1)}, f32[256,1024]{1,0:T(8,128)}, f32[13,1024]{1,0:T(8,128)}, f32[8,128]{1,0:T(8,128)}, f32[256,512]{1,0:T(8,128)}, /*index=5*/f32[1024,256]{1,0:T(8,128)}) custom-call(bf16[256,1024]{1,0:T(8,128)(2,1)} %bitcast.5, s32[1,1024]{1,0:T(1,128)} %refs_1_.2, s32[1,40]{1,0:T(1,128)} %refs_2_.2, ...), custom_call_target="tpu_custom_call" | custom-call | tf_op jit(solution)/shard_map/pallas_call | solution.py:1098
  173.1 7.2 %shard_map.237 = (f32[256,512]{1,0:T(8,128)}, f32[256,512]{1,0:T(8,128)}, f32[256,512]{1,0:T(8,128)}, bf16[256,512]{1,0:T(8,128)(2,1)}, f32[1024,256]{1,0:T(8,12...) custom-call(f32[8,128]{1,0:T(8,128)} %get-tuple-element.34.norm, ...), custom_call_target="tpu_custom_call" | custom-call | tf_op jit(solution)/shard_map/pallas_call | solution.py:1147
